TPU v7x, 32 devices: a whole 2x2x4 slice. The times are simulated.
32 devices in a mesh: rep: 16 (over z, x, core), shard: 2 (over y).
Axes of the slice: x: 2, y: 2, z: 4, core: 2. Of those that a mesh axis runs over, the one named last changes fastest.
Arguments:
- tokens: bfloat16 [4096, 1024], P(('rep', 'shard')), may hold values from -6 to 6
- cotangent: bfloat16 [4096, 1024], P(('rep', 'shard')), may hold values from -6 to 6
- segment_ids: int32 [4096], P(('rep', 'shard')), may hold values from -1 to 7, as said below
- flat_weights: float32 [12595200], P('shard')
- first_moment: float32 [12595200], P('shard'), may hold values from -1.2 to 1.2
- second_moment: float32 [12595200], P('shard'), may hold values from 0.5 to 2
Outputs:
- output: bfloat16 [4096, 1024], P(('rep', 'shard'))
- input_grad: bfloat16 [4096, 1024], P(('rep', 'shard'))
- weight_grad: float32 [12595200], P('shard')
- new_weights: float32 [12595200], P('shard')
- new_first: float32 [12595200], P('shard')
- new_second: float32 [12595200], P('shard')
Inputs may be any that keep to these rules, and one draw needn't show every extreme that they name: `segment_ids`: within each device's 128 rows the live rows come first, numbered 0, 1, 2 ... by sequence and never falling, followed by padding rows of -1; every sequence and every live span is a multiple of 16 rows, and each device has at least a quarter of its rows live. In every draw some device's rows form a single sequence of 128 rows, and some device has 8 sequences.
All inputs are finite; a program needn't handle non-finite values.
Results may differ from a plain program's by a relative error of at most 0.012.
The roundings to bfloat16 on the way count: a program that leaves them out, or rounds other values in their place, can miss the bound.
Values may be sent and summed in bfloat16 or wider, within the bound.
A program may use at most 512 MiB of HBM per device.

v0:
```python
import math

import jax
import jax.numpy as jnp
from jax import lax
from jax.sharding import PartitionSpec as P

D = 1024
HEADS = 16
HD = 64
FF = 4096
STEP = 3


def shapes_list():
    width = HEADS * HD
    return [
        (D, width),
        (D, width),
        (D, width),
        (width, D),
        (D, FF),
        (FF, D),
        (width,),
        (width,),
        (D,),
        (D,),
        (D,),
        (FF,),
        (D,),
        (D,),
        (D,),
    ]


def unpack(flat_vec):
    pieces = []
    offset = 0
    for extent in shapes_list():
        amount = math.prod(extent)
        pieces.append(lax.slice_in_dim(flat_vec, offset, offset + amount).reshape(extent))
        offset = offset + amount
    return pieces


def layer_norm(values, gain, shift):
    center = values - jnp.mean(values, axis=1, keepdims=True)
    spread = lax.rsqrt(jnp.mean(center * center, axis=1, keepdims=True) + 1e-05)
    normed = center * spread
    return (normed * gain.astype(jnp.float32) + shift.astype(jnp.float32), normed, spread)


def norm_back(upstream, normed, spread, gain):
    scaled = upstream * gain.astype(jnp.float32)
    inner = (
        scaled
        - jnp.mean(scaled, axis=1, keepdims=True)
        - normed * jnp.mean(scaled * normed, axis=1, keepdims=True)
    )
    return (spread * inner, jnp.sum(upstream * normed, axis=0), jnp.sum(upstream, axis=0))


def gelu_pair(values):
    cdf_part = 0.5 * (1.0 + lax.erf(values * 0.5**0.5))
    density = jnp.exp(-0.5 * values * values) * (2.0 * math.pi) ** (-0.5)
    return (values * cdf_part, cdf_part + values * density)


def heads_of(matrix):
    return matrix.reshape(matrix.shape[0], HEADS, HD)


def scores_of(query, keys, allowed):
    raw = jnp.einsum(
        "qhd,khd->hqk", heads_of(query), heads_of(keys), preferred_element_type=jnp.float32
    ) * HD ** (-0.5)
    return jnp.where(allowed[None, :, :], raw, -1e30)


def forward_pass(tokens, segment, params):
    (
        query_weight,
        key_weight,
        value_weight,
        output_weight,
        inner_weight,
        outer_weight,
        query_bias,
        value_bias,
        output_bias,
        first_gain,
        first_shift,
        inner_bias,
        outer_bias,
        second_gain,
        second_shift,
    ) = params
    rows = tokens.shape[0]
    residual = tokens.astype(jnp.float32)
    query = (
        jnp.dot(tokens, query_weight, preferred_element_type=jnp.float32)
        + query_bias.astype(jnp.float32)
    ).astype(jnp.bfloat16)
    keys = jnp.dot(tokens, key_weight, preferred_element_type=jnp.float32).astype(jnp.bfloat16)
    values = (
        jnp.dot(tokens, value_weight, preferred_element_type=jnp.float32)
        + value_bias.astype(jnp.float32)
    ).astype(jnp.bfloat16)
    allowed = segment[:, None] == segment[None, :]
    scores = scores_of(query, keys, allowed)
    row_max = jnp.max(scores, axis=2, keepdims=True)
    expo = jnp.exp(scores - row_max)
    row_sum = jnp.sum(expo, axis=2, keepdims=True)
    log_sum = row_max + jnp.log(row_sum)
    attn_prob = (expo / row_sum).astype(jnp.bfloat16)
    context = (
        jnp.einsum("hqk,khd->qhd", attn_prob, heads_of(values), preferred_element_type=jnp.float32)
        .reshape(rows, HEADS * HD)
        .astype(jnp.bfloat16)
    )
    attended = jnp.dot(
        context, output_weight, preferred_element_type=jnp.float32
    ) + output_bias.astype(jnp.float32)
    first_norm, first_normed, first_spread = layer_norm(
        residual + attended, first_gain, first_shift
    )
    first_round = first_norm.astype(jnp.bfloat16)
    inner_pre = jnp.dot(
        first_round, inner_weight, preferred_element_type=jnp.float32
    ) + inner_bias.astype(jnp.float32)
    inner_act, inner_slope = gelu_pair(inner_pre)
    inner_round = inner_act.astype(jnp.bfloat16)
    outer = jnp.dot(
        inner_round, outer_weight, preferred_element_type=jnp.float32
    ) + outer_bias.astype(jnp.float32)
    second_norm, second_normed, second_spread = layer_norm(
        first_norm + outer, second_gain, second_shift
    )
    live = (segment >= 0)[:, None]
    output = jnp.where(live, second_norm, residual).astype(jnp.bfloat16)
    saved = (
        query,
        keys,
        values,
        allowed,
        log_sum,
        context,
        first_normed,
        first_spread,
        first_round,
        inner_slope,
        inner_round,
        second_normed,
        second_spread,
        live,
    )
    return (output, saved)


def backward_pass(tokens, cotangent, saved, params):
    (
        query_weight,
        key_weight,
        value_weight,
        output_weight,
        inner_weight,
        outer_weight,
        query_bias,
        value_bias,
        output_bias,
        first_gain,
        first_shift,
        inner_bias,
        outer_bias,
        second_gain,
        second_shift,
    ) = params
    (
        query,
        keys,
        values,
        allowed,
        log_sum,
        context,
        first_normed,
        first_spread,
        first_round,
        inner_slope,
        inner_round,
        second_normed,
        second_spread,
        live,
    ) = saved
    rows = tokens.shape[0]
    upstream = jnp.where(live, cotangent.astype(jnp.float32), 0.0)
    back_second, grad_second_gain, grad_second_shift = norm_back(
        upstream, second_normed, second_spread, second_gain
    )
    back_second_round = back_second.astype(jnp.bfloat16)
    grad_outer_weight = jnp.dot(
        inner_round.T, back_second_round, preferred_element_type=jnp.float32
    )
    grad_outer_bias = jnp.sum(back_second, axis=0)
    back_inner = (
        jnp.dot(back_second_round, outer_weight.T, preferred_element_type=jnp.float32) * inner_slope
    )
    back_inner_round = back_inner.astype(jnp.bfloat16)
    grad_inner_weight = jnp.dot(first_round.T, back_inner_round, preferred_element_type=jnp.float32)
    grad_inner_bias = jnp.sum(back_inner, axis=0)
    back_first_out = back_second + jnp.dot(
        back_inner_round, inner_weight.T, preferred_element_type=jnp.float32
    )
    back_first, grad_first_gain, grad_first_shift = norm_back(
        back_first_out, first_normed, first_spread, first_gain
    )
    back_first_round = back_first.astype(jnp.bfloat16)
    grad_output_weight = jnp.dot(context.T, back_first_round, preferred_element_type=jnp.float32)
    grad_output_bias = jnp.sum(back_first, axis=0)
    back_context = jnp.dot(
        back_first_round, output_weight.T, preferred_element_type=jnp.float32
    ).astype(jnp.bfloat16)
    prob_again = jnp.exp(scores_of(query, keys, allowed) - log_sum)
    prob_round = prob_again.astype(jnp.bfloat16)
    back_values = jnp.einsum(
        "hqk,qhd->khd", prob_round, heads_of(back_context), preferred_element_type=jnp.float32
    ).reshape(rows, HEADS * HD)
    back_prob = jnp.einsum(
        "qhd,khd->hqk", heads_of(back_context), heads_of(values), preferred_element_type=jnp.float32
    )
    delta_rows = jnp.sum(
        heads_of(back_context).astype(jnp.float32) * heads_of(context).astype(jnp.float32), axis=2
    ).T
    back_scores = (prob_again * (back_prob - delta_rows[:, :, None]) * HD ** (-0.5)).astype(
        jnp.bfloat16
    )
    back_query = jnp.einsum(
        "hqk,khd->qhd", back_scores, heads_of(keys), preferred_element_type=jnp.float32
    ).reshape(rows, HEADS * HD)
    back_keys = jnp.einsum(
        "hqk,qhd->khd", back_scores, heads_of(query), preferred_element_type=jnp.float32
    ).reshape(rows, HEADS * HD)
    query_round = back_query.astype(jnp.bfloat16)
    keys_round = back_keys.astype(jnp.bfloat16)
    values_round = back_values.astype(jnp.bfloat16)
    grad_query_weight = jnp.dot(tokens.T, query_round, preferred_element_type=jnp.float32)
    grad_key_weight = jnp.dot(tokens.T, keys_round, preferred_element_type=jnp.float32)
    grad_value_weight = jnp.dot(tokens.T, values_round, preferred_element_type=jnp.float32)
    grad_query_bias = jnp.sum(back_query, axis=0)
    grad_value_bias = jnp.sum(back_values, axis=0)
    back_input = (
        back_first
        + jnp.dot(query_round, query_weight.T, preferred_element_type=jnp.float32)
        + jnp.dot(keys_round, key_weight.T, preferred_element_type=jnp.float32)
        + jnp.dot(values_round, value_weight.T, preferred_element_type=jnp.float32)
    )
    input_grad = jnp.where(live, back_input, cotangent.astype(jnp.float32)).astype(jnp.bfloat16)
    grad_list = [
        grad_query_weight,
        grad_key_weight,
        grad_value_weight,
        grad_output_weight,
        grad_inner_weight,
        grad_outer_weight,
        grad_query_bias,
        grad_value_bias,
        grad_output_bias,
        grad_first_gain,
        grad_first_shift,
        grad_inner_bias,
        grad_outer_bias,
        grad_second_gain,
        grad_second_shift,
    ]
    flat_grad = jnp.concatenate([member.reshape(-1).astype(jnp.bfloat16) for member in grad_list])
    return (input_grad, flat_grad)


def adamw(grad, weights, first, second):
    first_new = 0.9 * first + 0.1 * grad
    second_new = 0.98 * second + 0.02 * grad * grad
    first_hat = first_new / (1.0 - 0.9**STEP)
    second_hat = second_new / (1.0 - 0.98**STEP)
    weights_new = weights - 0.01 * (first_hat / (jnp.sqrt(second_hat) + 1e-06) + 0.01 * weights)
    return (weights_new, first_new, second_new)


def on_device(tokens, cotangent, segment_ids, flat_weights, first_moment, second_moment):
    gathered = lax.all_gather(flat_weights.astype(jnp.bfloat16), "shard", axis=0, tiled=True)
    params = unpack(gathered)
    output, saved = forward_pass(tokens, segment_ids, params)
    input_grad, local_grad = backward_pass(tokens, cotangent, saved, params)
    shards = lax.axis_size("shard")
    owned_len = local_grad.shape[0] // shards
    received = lax.all_to_all(
        local_grad.reshape(shards, owned_len), "shard", split_axis=0, concat_axis=0, tiled=True
    )
    group_part = jnp.sum(received.astype(jnp.float32), axis=0)
    weight_grad = lax.psum(group_part, "rep")
    new_weights, new_first, new_second = adamw(
        weight_grad, flat_weights, first_moment, second_moment
    )
    return (output, input_grad, weight_grad, new_weights, new_first, new_second)


def solution(mesh):
    return jax.shard_map(
        on_device,
        mesh=mesh,
        in_specs=(
            P(("rep", "shard"), None),
            P(("rep", "shard"), None),
            P(("rep", "shard")),
            P("shard"),
            P("shard"),
            P("shard"),
        ),
        out_specs=(
            P(("rep", "shard"), None),
            P(("rep", "shard"), None),
            P("shard"),
            P("shard"),
            P("shard"),
            P("shard"),
        ),
        check_vma=False,
    )
```

profile of v0, /device:TPU:0, one launch (start us, length us, event | category | flops | bytes accessed | tf_op | source)
XLA Modules:
  0.0 2178.3 jit_solution(18369592160568592269)
XLA Ops:
  7.2 14.5 convert_element_type.203
  22.4 298.6 %all-gather.2.cloned.1.call-done = bf16[12595200]{0:T(1024)(128)(2,1)} async-done(((bf16[6297600]{0:T(1024)(128)(2,1)}), bf16[12595200]{0:T(1024)(128)(2,1)}) %all-gather.2.cloned.1.call-update) | async-done | bytes 25190416 | tf_op jit(solution)/shard_map/all_gather | solution.py:288
  321.0 11.4 fusion.43
  332.5 13.3 slice.122
  345.7 13.3 slice.119
  359.0 6.0 fusion.44
  365.0 2.8 slice.106
  367.9 0.8 slice_convert_fusion.2
  369.3 4.3 slice.109
  373.6 2.0 fusion.14
  375.8 4.3 slice.112
  380.1 2.0 convolution_convert_fusion.3
  383.6 2.9 slice.114
  387.4 1.0 slice_convert_fusion
  388.4 4.9 convolution_add_fusion
  393.4 1.5 fusion.49
  395.5 1.0 fusion.40
  396.6 3.5 fusion.50
  400.1 3.0 multiply_reduce_fusion
  403.4 1.5 convolution_convert_fusion.1
  405.0 1.8 copy.40
  406.8 1.2 multiply_reduce_fusion.1
  408.0 1.8 fusion.8
  409.8 1.4 fusion.46
  411.2 2.2 convolution_convert_fusion
  413.4 2.5 fusion.45
  415.9 3.0 convert_bitcast_fusion.2
  418.9 5.9 convert_bitcast_fusion.1
  424.8 4.7 convert_bitcast_fusion
  429.5 0.7 convert_bitcast_fusion.5
  430.2 2.6 copy.45
  432.7 2.2 copy.54
  435.0 1.5 constant_dynamic-update-slice_fusion.13
  436.4 0.7 convert_bitcast_fusion.4
  437.1 2.9 copy.46
  440.1 3.5 copy.55
  444.3 2.6 copy.47
  446.8 3.6 copy.56
  450.4 3.5 copy.57
  454.0 9.6 copy.58
  463.6 9.1 copy.59
  472.8 1.5 constant_dynamic-update-slice_fusion.12
  474.3 3.8 constant_dynamic-update-slice_fusion.11
  478.1 3.2 constant_dynamic-update-slice_fusion.10
  481.3 4.2 constant_dynamic-update-slice_fusion.9
  485.4 0.7 slice-done.5
  486.2 3.6 constant_dynamic-update-slice_fusion.8
  495.0 299.9 %while.1 = (u32[]{:T(128)}, bf16[12595200]{0:T(1024)(128)(2,1)}, bf16[2,1,6297600]{2,1,0:T(2,128)(2,1)}, u32[]{}, u32[]{}) while((u32[]{:T(128)}, bf16[12595200]{0:T(1024)(128)(2,1)}, bf16[2,1,6297600]{2,1,0:T(2,128)(2,1)}, u32[]{}, u32[]{}) %tuple.54), condition=%wide.cond, body=%wide.body.sunk | while | flops 9 | bytes 62976164
  495.0 5.3 dynamic-slice.2
  500.3 144.6 %reshape_dynamic-update-slice_fusion.2 = bf16[2,1,6297600]{2,1,0:T(2,128)(2,1)} fusion(bf16[2,1,6297600]{2,1,0:T(2,128)(2,1)} %get-tuple-element.92, u32[]{:T(128)S(6)} %multiply.58, u32[]{:T(128)S(6)} %multiply.59, bf16[6297600]{0:T(1024)(128)(2,1)S(1)} %dynamic-slice.2), kind=kLoop, calls=%fused_computation.127.clone.1 | loop fusion | bytes 37785608
  644.9 5.3 dynamic-slice.2
  650.3 144.6 %reshape_dynamic-update-slice_fusion.2 = bf16[2,1,6297600]{2,1,0:T(2,128)(2,1)} fusion(bf16[2,1,6297600]{2,1,0:T(2,128)(2,1)} %get-tuple-element.92, u32[]{:T(128)S(6)} %multiply.58, u32[]{:T(128)S(6)} %multiply.59, bf16[6297600]{0:T(1024)(128)(2,1)S(1)} %dynamic-slice.2), kind=kLoop, calls=%fused_computation.127.clone.1 | loop fusion | bytes 37785608
  795.4 188.4 %reduce.3 = bf16[2,6297600]{1,0:T(2,128)(2,1)} reduce(bf16[2,1,6297600]{2,1,0:T(2,128)(2,1)} %get-tuple-element.10, bf16[]{:T(256)} %broadcast.121), dimensions={1}, to_apply=%get-tuple-element.10.reduce_sub_computation | reduce | bytes 50380800 | tf_op jit(solution)/shard_map/all_to_all | solution.py:294
  983.8 44.6 %reshape.208 = bf16[2,2,3148800]{2,1,0:T(2,128)(2,1)} reshape(bf16[2,6297600]{1,0:T(2,128)(2,1)} %reduce.3) | data formatting | bytes 50380800
  1028.4 297.9 %all_to_all.10 = bf16[2,2,3148800]{2,1,0:T(2,128)(2,1)} all-to-all(bf16[2,2,3148800]{2,1,0:T(2,128)(2,1)} %reshape.208), channel_id=1, replica_groups=mesh['rep'=16,'shard'=2] {'shard'}, dimensions={0} | all-to-all | bytes 50380800 | tf_op jit(solution)/shard_map/all_to_all | solution.py:294
  1326.3 56.2 %reshape.209 = bf16[2,1,6297600]{2,1,0:T(2,128)(2,1)} reshape(bf16[2,2,3148800]{2,1,0:T(2,128)(2,1)} %all_to_all.10) | data formatting | bytes 50380800
  1382.5 270.2 %convert_reduce_fusion = f32[6297600]{0:T(1024)} fusion(bf16[2,1,6297600]{2,1,0:T(2,128)(2,1)} %reshape.209), kind=kLoop, calls=%fused_computation | loop fusion | flops 18892800 | bytes 50380800 | tf_op jit(solution)/shard_map/reduce_sum | solution.py:297
  1652.7 1.0 copy-done.9
  1653.7 2.5 convolution_add_fusion.3
  1656.2 2.4 convolution_add_fusion.2
  1658.7 1.5 fusion.12
  1660.3 432.3 %all-reduce.2.cloned.1.call-done = f32[6297600]{0:T(1024)} async-done(((f32[6297600]{0:T(1024)}), f32[6297600]{0:T(1024)}) %all-reduce.2.cloned.1.call-update) | async-done | bytes 25190416 | tf_op jit(solution)/shard_map/psum | solution.py:298
  2092.6 59.4 %multiply_subtract_fusion = (f32[6297600]{0:T(1024)}, f32[6297600]{0:T(1024)}, f32[6297600]{0:T(1024)}) fusion(f32[6297600]{0:T(1024)} %param.9, f32[6297600]{0:T(1024)} %all-reduce.2.cloned.1.call-done, f32[6297600]{0:T(1024)} %param.10, f32[6297600]{0:T(1024)} %param.11), kind=kLoop, calls=%fused_computation.3 | loop fusion | flops 94464000 | bytes 176332800 | tf_op jit(solution)/shard_map/sub | solution.py:283
  2152.0 19.0 copy.84
  (109 shorter events, 11.4 us)
Async XLA Ops:
  7.2 313.9 %all-gather.2.cloned.1.call-start = ((), (), s32[]{:S(2)}) async-start(), calls=%async_computation.1 | async-start | bytes 37785600 | tf_op jit(solution)/shard_map/all_gather | solution.py:288
  21.7 0.7 copy-start.27
  21.7 2070.9 %all-reduce.2.cloned.1.call-start = ((), (), s32[]{:S(2)}) async-start(), calls=%async_computation.2 | async-start | bytes 50380800 | tf_op jit(solution)/shard_map/psum | solution.py:298
  22.4 373.2 %copy-start.25 = (pred[128]{0:T(512)(128)(4,1)}, pred[128]{0:T(512)(128)(4,1)S(1)}, u32[]{:S(2)}) copy-start(pred[128]{0:T(512)(128)(4,1)S(1)} %broadcast_compare_fusion.1) | copy-start | bytes 388
  359.0 9.7 copy-start.6
  367.8 14.3 copy-start.1
  369.3 13.6 copy-start.24
  375.8 10.8 copy-start.16
  382.3 4.3 copy-start.17
  382.7 1.0 copy-start.5
  383.6 9.7 copy-start.23
  386.6 1.8 copy-start.3
  387.2 6.2 slice-start.2
  388.4 5.0 slice-start.3
  393.4 1.7 copy-start.18
  395.5 4.6 slice-start
  396.6 3.5 copy-start.10
  396.6 3.5 slice-start.1
  400.0 3.1 copy-start.12
  400.1 3.4 copy-start.4
  403.4 21.4 copy-start.8
  406.8 12.1 copy-start.13
  409.8 15.0 copy-start.11
  411.2 18.3 copy-start.22
  429.5 7.0 copy-start.20
  434.9 8.6 copy-start.14
  463.6 9.3 copy-start.7
  472.8 8.4 copy-start
  478.1 7.4 slice-start.4
  481.3 4.9 slice-start.5
  1652.7 1.0 copy-start.9
  1652.7 3.6 copy-start.21
  1652.7 6.0 copy-start.2
  1652.7 6.0 copy-start.15
  1652.7 6.0 copy-start.19
  1652.7 6.0 copy-start.26
Sparse Core Ops, SparseCore 0:
  21.8 299.1 all-gather.1
  1652.8 439.6 all-reduce.1
where the time goes:
time: 2190 us; the launch traced here: 2180 us
  waiting for transfers between devices  731 us (33%)
  local copies, waits for them, and re-layouts  546 us (25%)
  other arithmetic  538 us (25%)
  blocking collectives  298 us (14%)
  matrix products  50.2 us (2%)
    unnamed x95, local copies, waits for them, and re-layouts  476 us
    psum x1, waiting for transfers between devices, on_device(): weight_grad = lax.psum(group_part, 'rep')  432 us
    all_gather x1, waiting for transfers between devices, on_device(): lax.all_gather(flat_weights.astype(jnp.bfloat16), 'shard', axis=0, tiled=...  299 us
    all_to_all x1, blocking collectives, on_device(): lax.all_to_all(local_grad.reshape(shards, owned_len), 'shard', split_axis...  298 us
    reduce_sum x1, other arithmetic, on_device(): group_part = jnp.sum(received.astype(jnp.float32), axis=0)  270 us
    all_to_all x1, other arithmetic, on_device(): lax.all_to_all(local_grad.reshape(shards, owned_len), 'shard', split_axis...  188 us
    sub x1, other arithmetic, adamw(): weights - 0.01 * (first_hat / (jnp.sqrt(second_hat) + 1e-06) + 0.01 * wei...  59.4 us
    slice x8, local copies, waits for them, and re-layouts, unpack(): lax.slice_in_dim(flat_vec, offset, offset + amount).reshape(extent)  58.2 us
  transfers between devices with their start and end apart: 2, of which 2 were waited for; matrix products, arithmetic and copies ran while one was open for 0% of the time, Pallas kernels for 0%

commit v1 on v0

--- a/solution.py
+++ b/solution.py
@@ -3,6 +3,8 @@
 import jax
 import jax.numpy as jnp
 from jax import lax
+from jax.experimental import pallas as pl
+from jax.experimental.pallas import tpu as pltpu
 from jax.sharding import PartitionSpec as P
 
 D = 1024
@@ -271,8 +273,7 @@
         grad_second_gain,
         grad_second_shift,
     ]
-    flat_grad = jnp.concatenate([member.reshape(-1).astype(jnp.bfloat16) for member in grad_list])
-    return (input_grad, flat_grad)
+    return (input_grad, grad_list)
 
 
 def adamw(grad, weights, first, second):
@@ -288,7 +289,8 @@
     gathered = lax.all_gather(flat_weights.astype(jnp.bfloat16), "shard", axis=0, tiled=True)
     params = unpack(gathered)
     output, saved = forward_pass(tokens, segment_ids, params)
-    input_grad, local_grad = backward_pass(tokens, cotangent, saved, params)
+    input_grad, grads = backward_pass(tokens, cotangent, saved, params)
+    local_grad = jnp.concatenate([member.reshape(-1).astype(jnp.bfloat16) for member in grads])
     shards = lax.axis_size("shard")
     owned_len = local_grad.shape[0] // shards
     received = lax.all_to_all(
@@ -302,9 +304,350 @@
     return (output, input_grad, weight_grad, new_weights, new_first, new_second)
 
 
+def flip(axis, bit):
+    here = lax.axis_index(axis)
+    return here + bit * (1 - 2 * (lax.rem(here // bit, 2)))
+
+
+def own_bit(axis, bit):
+    return lax.rem(lax.axis_index(axis) // bit, 2)
+
+
+LINKS = {
+    "core": ("rep", 1),
+    "x": ("rep", 2),
+    "z1": ("rep", 4),
+    "z2": ("rep", 8),
+    "y": ("shard", 1),
+}
+
+
+def partner(name):
+    axis, bit = LINKS[name]
+    return {axis: flip(axis, bit)}
+
+
+def side(name):
+    return own_bit(*LINKS[name])
+
+
+def greet(names):
+    barrier = pltpu.get_barrier_semaphore()
+    for name in names:
+        pl.semaphore_signal(
+            barrier, inc=1, device_id=partner(name), device_id_type=pl.DeviceIdType.MESH
+        )
+    pl.semaphore_wait(barrier, len(names))
+
+
+def send(source, target, send_sem, recv_sem, name):
+    copy = pltpu.make_async_remote_copy(
+        src_ref=source,
+        dst_ref=target,
+        send_sem=send_sem,
+        recv_sem=recv_sem,
+        device_id=partner(name),
+        device_id_type=pl.DeviceIdType.MESH,
+    )
+    copy.start()
+    return copy
+
+
+CHUNKS = 6
+
+
+def gather_kernel(own_ref, full_ref, send_sem, recv_sem, local_sem):
+    mine = side("y")
+    other = 1 - mine
+    quarter = side("x") * 2 + side("core")
+    across = (1 - side("x")) * 2 + side("core")
+    local = pltpu.make_async_copy(own_ref, full_ref.at[mine], local_sem)
+    greet(("y", "x", "core"))
+    first = []
+    for k in range(CHUNKS):
+        first.append(
+            send(
+                own_ref.at[quarter, k],
+                full_ref.at[mine, quarter, k],
+                send_sem.at[0, k],
+                recv_sem.at[0, k],
+                "y",
+            )
+        )
+    local.start()
+    second, third, fourth = [], [], []
+    for k in range(CHUNKS):
+        first[k].wait_recv()
+        block = full_ref.at[other, quarter, k]
+        second.append(send(block, block, send_sem.at[1, k], recv_sem.at[1, k], "x"))
+        third.append(send(block, block, send_sem.at[2, k], recv_sem.at[2, k], "core"))
+        if k > 0:
+            second[k - 1].wait_recv()
+            block = full_ref.at[other, across, k - 1]
+            fourth.append(
+                send(block, block, send_sem.at[3, k - 1], recv_sem.at[3, k - 1], "core")
+            )
+    last = CHUNKS - 1
+    second[last].wait_recv()
+    block = full_ref.at[other, across, last]
+    fourth.append(send(block, block, send_sem.at[3, last], recv_sem.at[3, last], "core"))
+    for k in range(CHUNKS):
+        third[k].wait_recv()
+        fourth[k].wait_recv()
+        first[k].wait_send()
+        second[k].wait_send()
+        third[k].wait_send()
+        fourth[k].wait_send()
+    local.wait()
+
+
+def gather_params(own):
+    rows = own.shape[0]
+    chunk = -(-rows // (4 * CHUNKS * 16)) * 16
+    padded = jnp.pad(own, ((0, 4 * CHUNKS * chunk - rows), (0, 0)))
+    full = pl.pallas_call(
+        gather_kernel,
+        out_shape=jax.ShapeDtypeStruct((2, 4, CHUNKS, chunk, 128), jnp.bfloat16),
+        in_specs=[pl.BlockSpec(memory_space=pl.ANY)],
+        out_specs=pl.BlockSpec(memory_space=pl.ANY),
+        scratch_shapes=[
+            pltpu.SemaphoreType.DMA((4, CHUNKS)),
+            pltpu.SemaphoreType.DMA((4, CHUNKS)),
+            pltpu.SemaphoreType.DMA,
+        ],
+        compiler_params=pltpu.CompilerParams(collective_id=0, has_side_effects=True),
+        name="gather_params",
+    )(padded.reshape(4, CHUNKS, chunk, 128))
+    return full.reshape(2, 4 * CHUNKS * chunk, 128)
+
+
+PLACE = (("x", "z1", "z2"), ("x", "z1", "z2"), ("z1", "x", "z2"))
+ORDER = (("y", "x", "z1", "z2"), ("x", "z1", "y", "z2"), ("z1", "y", "x", "z2"))
+SUM_LINKS = ("core", "y", "x", "z1", "z2")
+
+
+def index_of(done, part, name=None, swap=False):
+    entries = []
+    for dim in ("y",) + PLACE[part]:
+        if dim == name:
+            entries.append(1 - side(dim) if swap else side(dim))
+        elif dim in done:
+            entries.append(side(dim))
+        else:
+            entries.append(slice(None))
+    return tuple(entries)
+
+
+def add_blocks(shape, store, other):
+    total = math.prod(shape)
+
+    def body(i, carry):
+        index = []
+        rest = i
+        for extent in reversed(shape):
+            index.append(lax.rem(rest, extent))
+            rest = rest // extent
+        index = tuple(reversed(index))
+        here = store.at[index]
+        there = other.at[index]
+        here[...] = (here[...].astype(jnp.float32) + there[...].astype(jnp.float32)).astype(
+            jnp.bfloat16
+        )
+        return carry
+
+    lax.fori_loop(0, total, body, 0)
+
+
+def reduce_kernel(grad_ref, out_ref, own, *rest):
+    steps = len(ORDER[0])
+    landing = [rest[0:3]] + [rest[3 + 3 * t : 6 + 3 * t] for t in range(steps)]
+    send_sem, recv_sem, local_sem = rest[3 + 3 * steps :]
+    core = side("core")
+    greet(SUM_LINKS)
+    copies, local = [], []
+    for part in range(3):
+        copies.append(
+            send(
+                grad_ref.at[:, part, 1 - core],
+                landing[0][part],
+                send_sem.at[0, part],
+                recv_sem.at[0, part],
+                "core",
+            )
+        )
+        own_copy = pltpu.make_async_copy(
+            grad_ref.at[:, part, core], own.at[part], local_sem.at[part]
+        )
+        own_copy.start()
+        local.append(own_copy)
+    started = list(copies)
+    done = [(), (), ()]
+    last = [None, None, None]
+    for step in range(steps + 1):
+        for part in range(3):
+            copies[part].wait_recv()
+            if step == 0:
+                local[part].wait()
+                store = own.at[part]
+            else:
+                name = ORDER[part][step - 1]
+                store = own.at[(part,) + index_of(done[part], part, name)]
+                done[part] = done[part] + (name,)
+            source = landing[step][part]
+            lead = source.shape[:-2]
+            add_blocks(lead, store, source)
+            if step < steps:
+                name = ORDER[part][step]
+                copies[part] = send(
+                    own.at[(part,) + index_of(done[part], part, name, True)],
+                    landing[step + 1][part],
+                    send_sem.at[step + 1, part],
+                    recv_sem.at[step + 1, part],
+                    name,
+                )
+                started.append(copies[part])
+            else:
+                out_ref[part] = own[(part,) + index_of(done[part], part)]
+    for copy in started:
+        copy.wait_send()
+
+
+def reduce_scatter(rows):
+    piece, width = rows.shape[0] // 96, rows.shape[1]
+    scratch = [pltpu.VMEM((3, 2, 2, 2, 2, piece, width), jnp.bfloat16)]
+    scratch += [pltpu.VMEM((2, 2, 2, 2, piece, width), jnp.bfloat16)] * 3
+    for step in range(4):
+        for part in range(3):
+            used = ORDER[part][: step + 1]
+            lead = tuple(2 for dim in ("y",) + PLACE[part] if dim not in used)
+            scratch.append(pltpu.VMEM(lead + (piece, width), jnp.bfloat16))
+    scratch += [
+        pltpu.SemaphoreType.DMA((5, 3)),
+        pltpu.SemaphoreType.DMA((5, 3)),
+        pltpu.SemaphoreType.DMA((3,)),
+    ]
+    return pl.pallas_call(
+        reduce_kernel,
+        out_shape=jax.ShapeDtypeStruct((3, piece, width), jnp.bfloat16),
+        in_specs=[pl.BlockSpec(memory_space=pl.ANY)],
+        out_specs=pl.BlockSpec(memory_space=pltpu.VMEM),
+        scratch_shapes=scratch,
+        compiler_params=pltpu.CompilerParams(
+            collective_id=1, has_side_effects=True, vmem_limit_bytes=56 * 2**20
+        ),
+        name="reduce_scatter",
+    )(rows.reshape(2, 3, 2, 2, 2, 2, piece, width))
+
+
+SPREAD = (("z2", "z1", "x", "core"), ("z2", "x", "z1", "core"), ("x", "z2", "z1", "core"))
+
+
+def spread_kernel(piece_ref, full_ref, send_sem, recv_sem, local_sem):
+    def index(part, done):
+        return (part,) + tuple(
+            slice(None) if dim in done else side(dim) for dim in ("core",) + PLACE[part]
+        )
+
+    greet(("core", "x", "z1", "z2"))
+    copies, local, started = [], [], []
+    for part in range(3):
+        own_copy = pltpu.make_async_copy(
+            piece_ref.at[part], full_ref.at[index(part, ())], local_sem.at[part]
+        )
+        own_copy.start()
+        local.append(own_copy)
+    for part in range(3):
+        local[part].wait()
+    for step in range(4):
+        for part in range(3):
+            if step > 0:
+                copies[part].wait_recv()
+            block = full_ref.at[index(part, SPREAD[part][:step])]
+            copy = send(
+                block,
+                block,
+                send_sem.at[step, part],
+                recv_sem.at[step, part],
+                SPREAD[part][step],
+            )
+            started.append(copy)
+            if step > 0:
+                copies[part] = copy
+            else:
+                copies.append(copy)
+    for part in range(3):
+        copies[part].wait_recv()
+    for copy in started:
+        copy.wait_send()
+
+
+def spread(pieces):
+    rows = pieces.shape[1]
+    full = pl.pallas_call(
+        spread_kernel,
+        out_shape=jax.ShapeDtypeStruct((3, 2, 2, 2, 2, rows, 128), jnp.bfloat16),
+        in_specs=[pl.BlockSpec(memory_space=pl.ANY)],
+        out_specs=pl.BlockSpec(memory_space=pl.ANY),
+        scratch_shapes=[
+            pltpu.SemaphoreType.DMA((4, 3)),
+            pltpu.SemaphoreType.DMA((4, 3)),
+            pltpu.SemaphoreType.DMA((3,)),
+        ],
+        compiler_params=pltpu.CompilerParams(collective_id=2, has_side_effects=True),
+        name="spread",
+    )(pieces)
+    return full.reshape(3 * 16 * rows, 128)
+
+
+def unpack_pair(full, owned_rows):
+    pieces = []
+    offset = 0
+    for extent in shapes_list():
+        amount = math.prod(extent) // 128
+        members = []
+        for shard in range(2):
+            low = max(offset - shard * owned_rows, 0)
+            high = min(offset + amount - shard * owned_rows, owned_rows)
+            if high > low:
+                members.append(full[shard, low:high])
+        member = members[0] if len(members) == 1 else jnp.concatenate(members)
+        pieces.append(member.reshape(extent))
+        offset = offset + amount
+    return pieces
+
+
+def on_device_pair(tokens, cotangent, segment_ids, flat_weights, first_moment, second_moment):
+    owned = flat_weights.shape[0]
+    full = gather_params(flat_weights.reshape(owned // 128, 128).astype(jnp.bfloat16))
+    params = unpack_pair(full, owned // 128)
+    output, saved = forward_pass(tokens, segment_ids, params)
+    input_grad, grads = backward_pass(tokens, cotangent, saved, params)
+    rounded = [member.astype(jnp.bfloat16) for member in grads]
+    rows = jnp.concatenate([member.reshape(-1, D) for member in rounded[:6]])
+    half = rows.shape[0] // 2
+    vectors = jnp.concatenate(rounded[6:])
+    over = owned - half * D
+    tail = jnp.concatenate([rows[half : half + over // D].reshape(-1), vectors])
+    tail = lax.optimization_barrier(lax.psum(tail.astype(jnp.float32), ("rep", "shard")))
+    pieces = reduce_scatter(rows)
+    main = spread(pieces.reshape(3, -1, 128))
+    first_shard = lax.axis_index("shard") == 0
+    fill = jnp.zeros((vectors.shape[0] - over,), jnp.float32)
+    tail = jnp.where(first_shard, jnp.concatenate([tail[:over], fill]), tail[over:])
+    joined = jnp.concatenate([main, tail.astype(jnp.bfloat16).reshape(-1, 128)])
+    start = jnp.where(first_shard, 0, over // 128)
+    weight_grad = lax.dynamic_slice_in_dim(joined, start, owned // 128).astype(jnp.float32)
+    weight_grad = weight_grad.reshape(owned)
+    new_weights, new_first, new_second = adamw(
+        weight_grad, flat_weights, first_moment, second_moment
+    )
+    return (output, input_grad, weight_grad, new_weights, new_first, new_second)
+
+
 def solution(mesh):
+    paired = mesh.shape["shard"] == 2 and mesh.shape["rep"] == 16
     return jax.shard_map(
-        on_device,
+        on_device_pair if paired else on_device,
         mesh=mesh,
         in_specs=(
             P(("rep", "shard"), None),

time: 2190 us -> 963 us (0.44)
  waiting for transfers between devices: 731 us -> 0 us
  Pallas kernels: 0 us -> 647 us
  local copies, waits for them, and re-layouts: 546 us -> 91.7 us
  other arithmetic: 538 us -> 111 us
  blocking collectives: 298 us -> 40.5 us
    pallas_call x0 -> x3, Pallas kernels: none -> 647 us  [the longest x1 389 us: gather_params(): pl.pallas_call(gather_kernel, out_shape=jax.ShapeDtypeStruct((2, 4, CHUNK...]
    unnamed x95 -> x48, local copies, waits for them, and re-layouts: 476 us -> 9.43 us
    psum x1 -> x0, waiting for transfers between devices: 432 us -> none  [on_device(): weight_grad = lax.psum(group_part, 'rep')]
    all_gather x1 -> x0, waiting for transfers between devices: 299 us -> none  [on_device(): lax.all_gather(flat_weights.astype(jnp.bfloat16), 'shard', axis=0, tiled=...]
    all_to_all x1 -> x0, blocking collectives: 298 us -> none  [on_device(): lax.all_to_all(local_grad.reshape(shards, owned_len), 'shard', split_axis...]
    reduce_sum x1 -> x0, other arithmetic: 270 us -> none  [on_device(): group_part = jnp.sum(received.astype(jnp.float32), axis=0)]
    all_to_all x1 -> x0, other arithmetic: 188 us -> none  [on_device(): lax.all_to_all(local_grad.reshape(shards, owned_len), 'shard', split_axis...]
    slice x8 -> x3, local copies, waits for them, and re-layouts: 58.2 us -> 13.5 us  [the longest x2 12.8 us: unpack_pair(): members.append(full[shard, low:high])]
  transfers between devices with their start and end apart: 2 -> 0, of which waited for: 2 -> 0; matrix products, arithmetic and copies ran while one was open for 0% -> 0% of each run, Pallas kernels for 0% -> 0%
where the time goes in v1:
time: 963 us; the launch traced here: 953 us
  Pallas kernels  647 us (67%)
  other arithmetic  111 us (12%)
  local copies, waits for them, and re-layouts  91.7 us (10%)
  matrix products  61.4 us (6%)
  blocking collectives  40.5 us (4%)
    pallas_call x1, Pallas kernels, gather_params(): pl.pallas_call(gather_kernel, out_shape=jax.ShapeDtypeStruct((2, 4, CHUNK...  389 us
    pallas_call x1, Pallas kernels, reduce_scatter(): pl.pallas_call(reduce_kernel, out_shape=jax.ShapeDtypeStruct((3, piece, w...  139 us
    pallas_call x1, Pallas kernels, spread(): pl.pallas_call(spread_kernel, out_shape=jax.ShapeDtypeStruct((3, 2, 2, 2,...  119 us
    sub x1, other arithmetic, adamw(): weights - 0.01 * (first_hat / (jnp.sqrt(second_hat) + 1e-06) + 0.01 * wei...  65.2 us
    psum x1, blocking collectives, on_device_pair(): lax.psum(tail.astype(jnp.float32), ('rep', 'shard'))  40.5 us
    concatenate x1, other arithmetic, unpack_pair(): member = members[0] if len(members) == 1 else jnp.concatenate(members)  30.5 us
    another operation x5, local copies, waits for them, and re-layouts, unpack_pair(): pieces.append(member.reshape(extent))  27 us

profile of v1, /device:TPU:0, one launch (start us, length us, event | category | flops | bytes accessed | tf_op | source)
XLA Modules:
  0.0 953.4 jit_solution(11486712672622209013)
XLA Ops:
  0.6 0.7 broadcast_compare_fusion.1
  1.3 0.8 broadcast_compare_fusion
  2.1 9.5 convert_bitcast_fusion
  11.6 5.0 pad.5
  16.6 388.7 %gather_params.1 = bf16[2,4,6,2064,128]{4,3,2,1,0:T(8,128)(2,1)} custom-call(bf16[4,6,2064,128]{3,2,1,0:T(8,128)(2,1)} %bitcast.142), custom_call_target="tpu_custom_call" | custom-call | tf_op jit(solution)/shard_map/gather_params/pallas_call | solution.py:408
  405.3 0.7 fusion.42
  406.0 0.7 fusion.44
  406.7 2.4 slice_bitcast_fusion.1
  409.1 3.0 slice_bitcast_fusion
  412.1 30.5 %pad_maximum_fusion = bf16[32768,128]{1,0:T(8,128)(2,1)} fusion(bf16[16336,128]{1,0:T(8,128)(2,1)S(1)} %slice_bitcast_fusion.1, bf16[16432,128]{1,0:T(8,128)(2,1)S(1)} %slice_bitcast_fusion), kind=kLoop, calls=%fused_computation.10 | loop fusion | flops 16777216 | bytes 16777216 | tf_op jit(solution)/shard_map/concatenate | solution.py:613
  442.6 13.3 %reshape.246 = bf16[1024,4096]{1,0:T(8,128)(2,1)} reshape(bf16[32768,128]{1,0:T(8,128)(2,1)} %pad_maximum_fusion) | data formatting | bytes 16777216 | tf_op jit(solution)/shard_map/reshape | solution.py:614
  455.8 7.1 slice.101
  462.9 5.7 fusion.58
  468.6 13.3 %reshape_squeeze.28 = bf16[4096,1024]{1,0:T(8,128)(2,1)} reshape(bf16[1,32768,128]{2,1,0:T(8,128)(2,1)} %slice.101) | data formatting | bytes 16777216 | tf_op jit(solution)/shard_map/reshape;squeeze | solution.py:614
  481.9 2.3 reshape_squeeze.13
  484.2 2.8 reshape_squeeze.12
  487.0 1.5 convolution_convert_fusion.4
  488.5 4.3 reshape_squeeze.11
  492.8 2.4 fusion.17
  495.2 0.7 copy-done.12
  495.9 1.3 fusion.61
  497.2 0.2 fusion.18
  497.4 4.3 reshape_squeeze.10
  501.8 2.5 fusion.16
  504.3 0.3 convolution_convert_fusion.3
  504.6 0.5 fusion.62
  505.2 0.2 multiply_reduce_fusion.4
  505.4 0.0 slice-start.3
  505.4 4.9 convolution_add_fusion
  510.3 0.8 slice-done.3
  511.1 1.5 fusion.63
  512.6 0.2 multiply_reduce_fusion.3
  512.8 0.3 fusion.30
  513.2 0.0 slice-start
  513.2 1.0 fusion.55
  514.2 3.5 fusion.64
  517.7 3.0 multiply_reduce_fusion
  520.8 0.2 fusion.57
  521.0 1.5 convolution_convert_fusion.2
  522.6 1.8 copy.13
  524.4 1.1 multiply_reduce_fusion.1
  525.5 2.6 fusion.11
  528.1 2.5 fusion.59
  530.6 0.1 convert_element_type.335
  530.7 2.3 convolution_convert_fusion.1
  533.0 2.1 fusion.60
  535.1 0.1 convert_element_type.333
  535.2 2.6 convolution_add_fusion.3
  537.8 2.5 convolution_add_fusion.2
  540.3 3.2 fusion.15
  543.5 5.9 convolution_convert_fusion
  549.4 13.9 %reshape.248 = bf16[4096,1024]{1,0:T(8,128)(2,1)} reshape(bf16[1024,4096]{1,0:T(8,128)(2,1)} %convolution_convert_fusion) | data formatting | bytes 16777216 | tf_op jit(solution)/shard_map/reshape | solution.py:626
  563.3 0.7 slice.105
  564.2 40.5 %psum.7 = bf16[18432]{0:T(1024)(128)(2,1)S(1)} all-reduce(bf16[18432]{0:T(1024)(128)(2,1)S(1)} %constant_dynamic-update-slice_fusion.3), channel_id=1, replica_groups=mesh['rep'=16,'shard'=2] {'rep','shard'}, use_global_device_ids=true, to_apply=%region_20.21 | all-reduce | flops 18432 | bytes 73728 | tf_op jit(solution)/shard_map/psum | solution.py:631
  604.7 3.0 bitcast_dynamic-update-slice_fusion.2
  607.8 2.1 bitcast_dynamic-update-slice_fusion.1
  609.8 2.1 bitcast_dynamic-update-slice_fusion
  611.9 3.0 convert_dynamic-update-slice_fusion.1
  614.9 7.8 constant_dynamic-update-slice_fusion
  622.7 4.7 convert_dynamic-update-slice_fusion
  627.4 139.5 %reduce_scatter.1 = bf16[3,128,1024]{2,1,0:T(8,128)(2,1)} custom-call(bf16[2,3,2,2,2,2,128,1024]{7,6,5,4,3,2,1,0:T(8,128)(2,1)} %bitcast.38.grad_ref), custom_call_target="tpu_custom_call" | custom-call | tf_op jit(solution)/shard_map/reduce_scatter/pallas_call | solution.py:529
  766.9 2.2 reshape.250.piece_ref
  769.1 118.7 %spread.1 = bf16[3,2,2,2,2,1024,128]{6,5,4,3,2,1,0:T(8,128)(2,1)} custom-call(bf16[3,1024,128]{2,1,0:T(8,128)(2,1)} %reshape.250.piece_ref), custom_call_target="tpu_custom_call" | custom-call | tf_op jit(solution)/shard_map/spread/pallas_call | solution.py:586
  887.7 65.2 %multiply_subtract_fusion = (f32[6297600]{0:T(1024)}, f32[6297600]{0:T(1024)}, f32[6297600]{0:T(1024)}, f32[6297600]{0:T(1024)}) fusion(f32[6297600]{0:T(1024)} %param.9, f32[6297600]{0:T(1024)} %param.10, f32[6297600]{0:T(1024)} %param.11, s32[]{:T(128)S(6)} %select_n.37, bf16[96,128]{1,0:T(8,128)(2,1)S(1)} %fusion.41, bf16[49152,128]{1,0:T(8,128)(2,1)} %bitcast.143), kind=kLoop, calls=%fused_computation.2 | loop fusion | flops 125952000 | bytes 188940288 | tf_op jit(solution)/shard_map/sub | solution.py:284
  (56 shorter events, 0.3 us)
Async XLA Ops:
  481.9 5.1 copy-start.3
  487.0 14.7 %copy-start = (bf16[1024,1024]{1,0:T(8,128)(2,1)}, bf16[1024,1024]{1,0:T(8,128)(2,1)S(1)}, u32[]{:S(2)}) copy-start(bf16[1024,1024]{1,0:T(8,128)(2,1)S(1)} %reshape_squeeze.12) | copy-start | bytes 6291460
  495.2 0.7 copy-start.12
  497.2 7.4 copy-start.2
  501.7 2.9 copy-start.1
  504.3 1.1 copy-start.13
  504.6 0.8 copy-start.11
  505.2 5.2 slice-start.2
  505.4 5.7 slice-start.3
  511.1 1.7 copy-start.9
  513.2 4.5 slice-start
  514.2 3.5 copy-start.4
  514.2 3.5 slice-start.1
  517.7 4.9 copy-start.6
  535.2 8.3 copy-start.7
  549.4 55.3 %copy-start.14 = (pred[12288]{0:T(1024)(128)(4,1)S(1)}, pred[12288]{0:T(1024)(128)(4,1)}, u32[]{:S(2)}) copy-start(pred[12288]{0:T(1024)(128)(4,1)} %constant.56.clone.1) | copy-start | bytes 36868
  549.4 58.4 %copy-start.10 = (bf16[16,64,128]{2,1,0:T(8,128)(2,1)S(1)}, bf16[16,64,128]{2,1,0:T(8,128)(2,1)}, u32[]{:S(2)}) copy-start(bf16[16,64,128]{2,1,0:T(8,128)(2,1)} %convolution_convert_fusion.1) | copy-start | bytes 786436
  549.4 60.4 %copy-start.8 = (bf16[128,16,64]{0,2,1:T(8,128)(2,1)S(1)}, bf16[128,16,64]{0,2,1:T(8,128)(2,1)}, u32[]{:S(2)}) copy-start(bf16[128,16,64]{0,2,1:T(8,128)(2,1)} %get-tuple-element.36) | copy-start | bytes 786436
  614.9 7.8 copy-start.5

commit v2 on v1

--- a/solution.py
+++ b/solution.py
@@ -356,41 +356,72 @@
 CHUNKS = 6
 
 
-def gather_kernel(own_ref, full_ref, send_sem, recv_sem, local_sem):
+def gather_kernel(own_ref, full_ref, send_sem, recv_sem):
+    owned = own_ref.shape[0]
+    chunk = owned // (4 * CHUNKS * 16) * 16
+    extra = owned - 4 * CHUNKS * chunk
     mine = side("y")
     other = 1 - mine
     quarter = side("x") * 2 + side("core")
     across = (1 - side("x")) * 2 + side("core")
-    local = pltpu.make_async_copy(own_ref, full_ref.at[mine], local_sem)
+
+    def place(part, k):
+        return (part * CHUNKS + k) * chunk
+
+    def here(start, size):
+        return own_ref.at[pl.ds(pl.multiple_of(start, 16), size)]
+
+    def there(shard, start, size):
+        return full_ref.at[pl.ds(pl.multiple_of(shard * owned + start, 16), size)]
+
     greet(("y", "x", "core"))
     first = []
     for k in range(CHUNKS):
+        start = place(quarter, k)
         first.append(
             send(
-                own_ref.at[quarter, k],
-                full_ref.at[mine, quarter, k],
+                here(start, chunk),
+                there(mine, start, chunk),
                 send_sem.at[0, k],
                 recv_sem.at[0, k],
                 "y",
             )
         )
-    local.start()
+    rest = 4 * CHUNKS * chunk
+    final = None
+    if extra:
+        final = send(
+            here(rest, extra),
+            there(mine, rest, extra),
+            send_sem.at[0, CHUNKS],
+            recv_sem.at[0, CHUNKS],
+            "y",
+        )
+    step = owned // (16 * 25) * 16 if owned % (16 * 25) == 0 else 16
+
+    def keep(i, carry):
+        start = pl.multiple_of(i * step, 16)
+        target = pl.multiple_of(mine * owned + i * step, 16)
+        full_ref[pl.ds(target, step), :] = own_ref[pl.ds(start, step), :]
+        return carry
+
+    lax.fori_loop(0, owned // step, keep, 0)
     second, third, fourth = [], [], []
+
+    def pass_on(part, k, row, name):
+        block = there(other, place(part, k), chunk)
+        return send(block, block, send_sem.at[row, k], recv_sem.at[row, k], name)
+
     for k in range(CHUNKS):
         first[k].wait_recv()
-        block = full_ref.at[other, quarter, k]
-        second.append(send(block, block, send_sem.at[1, k], recv_sem.at[1, k], "x"))
-        third.append(send(block, block, send_sem.at[2, k], recv_sem.at[2, k], "core"))
+        second.append(pass_on(quarter, k, 1, "x"))
+        third.append(pass_on(quarter, k, 2, "core"))
         if k > 0:
             second[k - 1].wait_recv()
-            block = full_ref.at[other, across, k - 1]
-            fourth.append(
-                send(block, block, send_sem.at[3, k - 1], recv_sem.at[3, k - 1], "core")
-            )
+            fourth.append(pass_on(across, k - 1, 3, "core"))
     last = CHUNKS - 1
     second[last].wait_recv()
-    block = full_ref.at[other, across, last]
-    fourth.append(send(block, block, send_sem.at[3, last], recv_sem.at[3, last], "core"))
+    fourth.append(pass_on(across, last, 3, "core"))
     for k in range(CHUNKS):
         third[k].wait_recv()
         fourth[k].wait_recv()
@@ -398,27 +429,25 @@
         second[k].wait_send()
         third[k].wait_send()
         fourth[k].wait_send()
-    local.wait()
+    if extra:
+        final.wait()
 
 
 def gather_params(own):
-    rows = own.shape[0]
-    chunk = -(-rows // (4 * CHUNKS * 16)) * 16
-    padded = jnp.pad(own, ((0, 4 * CHUNKS * chunk - rows), (0, 0)))
-    full = pl.pallas_call(
+    return pl.pallas_call(
         gather_kernel,
-        out_shape=jax.ShapeDtypeStruct((2, 4, CHUNKS, chunk, 128), jnp.bfloat16),
-        in_specs=[pl.BlockSpec(memory_space=pl.ANY)],
-        out_specs=pl.BlockSpec(memory_space=pl.ANY),
+        out_shape=jax.ShapeDtypeStruct((2 * own.shape[0], 128), jnp.bfloat16),
+        in_specs=[pl.BlockSpec(memory_space=pltpu.VMEM)],
+        out_specs=pl.BlockSpec(memory_space=pltpu.VMEM),
         scratch_shapes=[
-            pltpu.SemaphoreType.DMA((4, CHUNKS)),
-            pltpu.SemaphoreType.DMA((4, CHUNKS)),
-            pltpu.SemaphoreType.DMA,
+            pltpu.SemaphoreType.DMA((4, CHUNKS + 1)),
+            pltpu.SemaphoreType.DMA((4, CHUNKS + 1)),
         ],
-        compiler_params=pltpu.CompilerParams(collective_id=0, has_side_effects=True),
+        compiler_params=pltpu.CompilerParams(
+            collective_id=0, has_side_effects=True, vmem_limit_bytes=56 * 2**20
+        ),
         name="gather_params",
-    )(padded.reshape(4, CHUNKS, chunk, 128))
-    return full.reshape(2, 4 * CHUNKS * chunk, 128)
+    )(own)
 
 
 PLACE = (("x", "z1", "z2"), ("x", "z1", "z2"), ("z1", "x", "z2"))
@@ -458,10 +487,22 @@
     lax.fori_loop(0, total, body, 0)
 
 
-def reduce_kernel(grad_ref, out_ref, own, *rest):
+def reduce_kernel(grad_ref, tail_ref, out_ref, total_ref, own, tail_sum, tail_in, *rest):
     steps = len(ORDER[0])
     landing = [rest[0:3]] + [rest[3 + 3 * t : 6 + 3 * t] for t in range(steps)]
-    send_sem, recv_sem, local_sem = rest[3 + 3 * steps :]
+    send_sem, recv_sem, local_sem, tail_send, tail_recv = rest[3 + 3 * steps :]
+
+    def tail_step(step):
+        copy = send(
+            tail_sum.at[step],
+            tail_in.at[step],
+            tail_send.at[step],
+            tail_recv.at[step],
+            SUM_LINKS[step],
+        )
+        started.append(copy)
+        return copy
+
     core = side("core")
     greet(SUM_LINKS)
     copies, local = [], []
@@ -481,8 +522,9 @@
         own_copy.start()
         local.append(own_copy)
     started = list(copies)
+    tail_sum[0] = tail_ref[...]
+    tail_copy = tail_step(0)
     done = [(), (), ()]
-    last = [None, None, None]
     for step in range(steps + 1):
         for part in range(3):
             copies[part].wait_recv()
@@ -508,13 +550,20 @@
                 started.append(copies[part])
             else:
                 out_ref[part] = own[(part,) + index_of(done[part], part)]
+        tail_copy.wait_recv()
+        if step < steps:
+            tail_sum[step + 1] = tail_sum[step] + tail_in[step]
+            tail_copy = tail_step(step + 1)
+        else:
+            total_ref[...] = tail_sum[step] + tail_in[step]
     for copy in started:
         copy.wait_send()
 
 
-def reduce_scatter(rows):
+def reduce_scatter(rows, tail):
     piece, width = rows.shape[0] // 96, rows.shape[1]
     scratch = [pltpu.VMEM((3, 2, 2, 2, 2, piece, width), jnp.bfloat16)]
+    scratch += [pltpu.VMEM((5,) + tail.shape, jnp.float32)] * 2
     scratch += [pltpu.VMEM((2, 2, 2, 2, piece, width), jnp.bfloat16)] * 3
     for step in range(4):
         for part in range(3):
@@ -525,39 +574,44 @@
         pltpu.SemaphoreType.DMA((5, 3)),
         pltpu.SemaphoreType.DMA((5, 3)),
         pltpu.SemaphoreType.DMA((3,)),
+        pltpu.SemaphoreType.DMA((5,)),
+        pltpu.SemaphoreType.DMA((5,)),
     ]
     return pl.pallas_call(
         reduce_kernel,
-        out_shape=jax.ShapeDtypeStruct((3, piece, width), jnp.bfloat16),
-        in_specs=[pl.BlockSpec(memory_space=pl.ANY)],
-        out_specs=pl.BlockSpec(memory_space=pltpu.VMEM),
+        out_shape=(
+            jax.ShapeDtypeStruct((3, piece, width), jnp.bfloat16),
+            jax.ShapeDtypeStruct(tail.shape, jnp.float32),
+        ),
+        in_specs=[
+            pl.BlockSpec(memory_space=pl.ANY),
+            pl.BlockSpec(memory_space=pltpu.VMEM),
+        ],
+        out_specs=(
+            pl.BlockSpec(memory_space=pltpu.VMEM),
+            pl.BlockSpec(memory_space=pltpu.VMEM),
+        ),
         scratch_shapes=scratch,
         compiler_params=pltpu.CompilerParams(
             collective_id=1, has_side_effects=True, vmem_limit_bytes=56 * 2**20
         ),
         name="reduce_scatter",
-    )(rows.reshape(2, 3, 2, 2, 2, 2, piece, width))
+    )(rows.reshape(2, 3, 2, 2, 2, 2, piece, width), tail)
 
 
 SPREAD = (("z2", "z1", "x", "core"), ("z2", "x", "z1", "core"), ("x", "z2", "z1", "core"))
 
 
-def spread_kernel(piece_ref, full_ref, send_sem, recv_sem, local_sem):
+def spread_kernel(piece_ref, full_ref, send_sem, recv_sem):
     def index(part, done):
         return (part,) + tuple(
             slice(None) if dim in done else side(dim) for dim in ("core",) + PLACE[part]
         )
 
     greet(("core", "x", "z1", "z2"))
-    copies, local, started = [], [], []
+    copies, started = [], []
     for part in range(3):
-        own_copy = pltpu.make_async_copy(
-            piece_ref.at[part], full_ref.at[index(part, ())], local_sem.at[part]
-        )
-        own_copy.start()
-        local.append(own_copy)
-    for part in range(3):
-        local[part].wait()
+        full_ref[index(part, ())] = piece_ref[part]
     for step in range(4):
         for part in range(3):
             if step > 0:
@@ -586,40 +640,24 @@
     full = pl.pallas_call(
         spread_kernel,
         out_shape=jax.ShapeDtypeStruct((3, 2, 2, 2, 2, rows, 128), jnp.bfloat16),
-        in_specs=[pl.BlockSpec(memory_space=pl.ANY)],
-        out_specs=pl.BlockSpec(memory_space=pl.ANY),
+        in_specs=[pl.BlockSpec(memory_space=pltpu.VMEM)],
+        out_specs=pl.BlockSpec(memory_space=pltpu.VMEM),
         scratch_shapes=[
             pltpu.SemaphoreType.DMA((4, 3)),
             pltpu.SemaphoreType.DMA((4, 3)),
-            pltpu.SemaphoreType.DMA((3,)),
         ],
-        compiler_params=pltpu.CompilerParams(collective_id=2, has_side_effects=True),
+        compiler_params=pltpu.CompilerParams(
+            collective_id=2, has_side_effects=True, vmem_limit_bytes=40 * 2**20
+        ),
         name="spread",
     )(pieces)
     return full.reshape(3 * 16 * rows, 128)
 
 
-def unpack_pair(full, owned_rows):
-    pieces = []
-    offset = 0
-    for extent in shapes_list():
-        amount = math.prod(extent) // 128
-        members = []
-        for shard in range(2):
-            low = max(offset - shard * owned_rows, 0)
-            high = min(offset + amount - shard * owned_rows, owned_rows)
-            if high > low:
-                members.append(full[shard, low:high])
-        member = members[0] if len(members) == 1 else jnp.concatenate(members)
-        pieces.append(member.reshape(extent))
-        offset = offset + amount
-    return pieces
-
-
 def on_device_pair(tokens, cotangent, segment_ids, flat_weights, first_moment, second_moment):
     owned = flat_weights.shape[0]
     full = gather_params(flat_weights.reshape(owned // 128, 128).astype(jnp.bfloat16))
-    params = unpack_pair(full, owned // 128)
+    params = unpack(full.reshape(-1))
     output, saved = forward_pass(tokens, segment_ids, params)
     input_grad, grads = backward_pass(tokens, cotangent, saved, params)
     rounded = [member.astype(jnp.bfloat16) for member in grads]
@@ -628,8 +666,8 @@
     vectors = jnp.concatenate(rounded[6:])
     over = owned - half * D
     tail = jnp.concatenate([rows[half : half + over // D].reshape(-1), vectors])
-    tail = lax.optimization_barrier(lax.psum(tail.astype(jnp.float32), ("rep", "shard")))
-    pieces = reduce_scatter(rows)
+    pieces, tail = reduce_scatter(rows, tail.astype(jnp.float32).reshape(-1, 128))
+    tail = tail.reshape(-1)
     main = spread(pieces.reshape(3, -1, 128))
     first_shard = lax.axis_index("shard") == 0
     fill = jnp.zeros((vectors.shape[0] - over,), jnp.float32)

time: 963 us -> 583 us (0.61)
  Pallas kernels: 647 us -> 336 us
  blocking collectives: 40.5 us -> 0 us
  other arithmetic: 111 us -> 87.4 us
    pallas_call x2, Pallas kernels: 528 us -> 245 us  [the longest x1 145 us: reduce_scatter(): pl.pallas_call(reduce_kernel, out_shape=(jax.ShapeDtypeStruct((3, piece,...]
    psum x1 -> x0, blocking collectives: 40.5 us -> none  [on_device_pair(): lax.psum(tail.astype(jnp.float32), ('rep', 'shard'))]
    concatenate x1 -> x0, other arithmetic: 30.5 us -> none  [unpack_pair(): member = members[0] if len(members) == 1 else jnp.concatenate(members)]
    another operation x5 -> x0, local copies, waits for them, and re-layouts: 27 us -> none  [unpack_pair(): pieces.append(member.reshape(extent))]
    pallas_call x1, Pallas kernels: 119 us -> 91.8 us  [spread(): pl.pallas_call(spread_kernel, out_shape=jax.ShapeDtypeStruct((3, 2, 2, 2,...]
    reshape x1 -> x6, local copies, waits for them, and re-layouts: 13.3 us -> 38.8 us  [unpack(): lax.slice_in_dim(flat_vec, offset, offset + amount).reshape(extent)]
where the time goes in v2:
time: 583 us; the launch traced here: 581 us
  Pallas kernels  336 us (58%)
  local copies, waits for them, and re-layouts  90.9 us (16%)
  other arithmetic  87.4 us (15%)
  matrix products  65 us (11%)
    pallas_call x1, Pallas kernels, reduce_scatter(): pl.pallas_call(reduce_kernel, out_shape=(jax.ShapeDtypeStruct((3, piece,...  145 us
    pallas_call x1, Pallas kernels, gather_params(): pl.pallas_call(gather_kernel, out_shape=jax.ShapeDtypeStruct((2 * own.sha...  99.7 us
    pallas_call x1, Pallas kernels, spread(): pl.pallas_call(spread_kernel, out_shape=jax.ShapeDtypeStruct((3, 2, 2, 2,...  91.8 us
    sub x1, other arithmetic, adamw(): weights - 0.01 * (first_hat / (jnp.sqrt(second_hat) + 1e-06) + 0.01 * wei...  65.2 us
    reshape x6, local copies, waits for them, and re-layouts, unpack(): lax.slice_in_dim(flat_vec, offset, offset + amount).reshape(extent)  38.8 us
    slice x2, local copies, waits for them, and re-layouts, unpack(): lax.slice_in_dim(flat_vec, offset, offset + amount).reshape(extent)  17.1 us
    convert_element_type x1, other arithmetic, on_device_pair(): flat_weights.reshape(owned // 128, 128).astype(jnp.bfloat16)  14.5 us
    reshape x1, local copies, waits for them, and re-layouts, on_device_pair(): rows = jnp.concatenate([member.reshape(-1, D) for member in rounded[:6]])  13.9 us

profile of v2, /device:TPU:0, one launch (start us, length us, event | category | flops | bytes accessed | tf_op | source)
XLA Modules:
  0.0 580.8 jit_solution(3614179064474837451)
XLA Ops:
  0.6 0.7 broadcast_compare_fusion.1
  1.3 0.8 broadcast_compare_fusion
  2.1 14.5 %convert_bitcast_fusion.own_ref = bf16[49200,128]{1,0:T(8,128)(2,1)} fusion(f32[6297600]{0:T(1024)} %param.9), kind=kLoop, calls=%fused_computation.9 | loop fusion | flops 6297600 | bytes 37785600 | tf_op jit(solution)/shard_map/convert_element_type | solution.py:659
  16.6 99.7 %gather_params.1 = bf16[98400,128]{1,0:T(8,128)(2,1)} custom-call(bf16[49200,128]{1,0:T(8,128)(2,1)} %convert_bitcast_fusion.own_ref), custom_call_target="tpu_custom_call" | custom-call | tf_op jit(solution)/shard_map/gather_params/pallas_call | solution.py:437
  116.3 0.7 bitcast_convert_fusion.1
  117.0 0.7 bitcast_convert_fusion.3
  117.7 5.7 fusion.50
  123.4 11.4 %fusion.49 = (bf16[32768,128]{1,0:T(8,128)(2,1)}, bf16[32768,128]{1,0:T(8,128)(2,1)}) fusion(bf16[98400,128]{1,0:T(8,128)(2,1)} %gather_params.1), kind=kLoop, calls=%fused_computation.125 | loop fusion | bytes 33554432 | tf_op jit(solution)/shard_map/slice | solution.py:43
  134.8 13.3 %reshape.270 = bf16[1024,4096]{1,0:T(8,128)(2,1)} reshape(bf16[32768,128]{1,0:T(8,128)(2,1)} %get-tuple-element.34) | data formatting | bytes 16777216 | tf_op jit(solution)/shard_map/reshape | solution.py:43
  148.1 2.3 reshape.269
  150.4 2.8 reshape.267
  153.2 0.4 convolution_convert_fusion.4
  153.7 1.0 copy.26
  154.7 4.2 reshape.265
  158.8 2.0 fusion.17
  160.9 0.8 copy.25
  161.7 1.4 fusion.53
  163.1 0.2 fusion.18
  163.3 3.0 reshape.263
  166.4 1.4 fusion.16
  167.7 1.8 copy.24
  169.5 1.3 convolution_convert_fusion.3
  170.8 2.2 fusion.54
  173.1 0.2 multiply_reduce_fusion.4
  173.3 4.7 convolution_add_fusion
  178.0 13.3 %reshape.271 = bf16[4096,1024]{1,0:T(8,128)(2,1)} reshape(bf16[32768,128]{1,0:T(8,128)(2,1)} %get-tuple-element.35) | data formatting | bytes 16777216 | tf_op jit(solution)/shard_map/reshape | solution.py:43
  191.3 5.0 fusion.55
  196.3 0.2 multiply_reduce_fusion.3
  196.6 0.3 fusion.30
  196.9 0.0 slice-start
  196.9 1.0 fusion.46
  198.0 3.5 fusion.56
  201.4 0.0 copy-start.9
  201.5 3.0 multiply_reduce_fusion
  204.5 0.2 fusion.48
  204.8 1.5 convolution_convert_fusion.2
  206.3 1.8 copy.28
  208.1 1.1 multiply_reduce_fusion.1
  209.2 2.6 fusion.11
  211.9 2.5 fusion.51
  214.3 0.1 convert_element_type.320
  214.4 2.3 convolution_convert_fusion.1
  216.7 2.1 fusion.52
  218.8 0.1 convert_element_type.318
  218.9 2.6 convolution_add_fusion.3
  221.5 2.5 convolution_add_fusion.2
  224.0 3.2 fusion.15
  227.2 5.9 %convolution_convert_fusion = bf16[1024,4096]{1,0:T(8,128)(2,1)} fusion(bf16[128,4096]{1,0:T(8,128)(2,1)S(1)} %copy-done.10, f32[128,1024]{1,0:T(8,128)S(1)} %get-tuple-element.48, f32[1024]{0:T(1024)S(1)} %get-tuple-element.29, f32[1024]{0:T(1024)S(1)} %get-tuple-element.30, f32[128]{0:T(128)S(1)} %add_rsqrt_fusion.1, f32[128]{0:T(128)S(1)} %broadcast_multiply_fusion.5), kind=kOutput, calls=%fused_computation.11 | convolution fusion | flops 1078591488 | bytes 9970688 | tf_op jit(solution)/shard_map/dot_general | solution.py:210
  233.1 13.9 %reshape.273 = bf16[4096,1024]{1,0:T(8,128)(2,1)} reshape(bf16[1024,4096]{1,0:T(8,128)(2,1)} %convolution_convert_fusion) | data formatting | bytes 16777216 | tf_op jit(solution)/shard_map/reshape | solution.py:664
  247.0 0.7 slice.95
  247.9 0.6 bitcast_convert_fusion.tail_ref
  248.6 3.0 bitcast_dynamic-update-slice_fusion.2
  251.6 2.1 bitcast_dynamic-update-slice_fusion.1
  253.7 2.1 bitcast_dynamic-update-slice_fusion
  255.7 3.0 convert_dynamic-update-slice_fusion.1
  258.7 7.8 %constant_dynamic-update-slice_fusion = bf16[12288,1024]{1,0:T(8,128)(2,1)} fusion(bf16[12288,1024]{1,0:T(8,128)(2,1)} %convert_dynamic-update-slice_fusion.1, bf16[4096,1024]{1,0:T(8,128)(2,1)} %reshape.273), kind=kLoop, calls=%fused_computation.93 | loop fusion | bytes 16777216
  266.5 4.7 convert_dynamic-update-slice_fusion
  271.2 145.0 %reduce_scatter.1 = (bf16[3,128,1024]{2,1,0:T(8,128)(2,1)}, f32[144,128]{1,0:T(8,128)}) custom-call(bf16[2,3,2,2,2,2,128,1024]{7,6,5,4,3,2,1,0:T(8,128)(2,1)} %bitcast.28.grad_ref, f32[144,128]{1,0:T(8,128)} %bitcast_convert_fusion.tail_ref), custom_call_target="tpu_custom_call" | custom-call | tf_op jit(solution)/shard_map/reduce_scatter/pallas_call | solution.py:580
  416.2 1.4 reshape.276.piece_ref
  417.7 0.7 slice_bitcast_fusion
  418.4 0.8 fusion.41
  419.2 91.8 %spread.1 = bf16[3,2,2,2,2,1024,128]{6,5,4,3,2,1,0:T(8,128)(2,1)S(1)} custom-call(bf16[3,1024,128]{2,1,0:T(8,128)(2,1)S(1)} %reshape.276.piece_ref), custom_call_target="tpu_custom_call" | custom-call | tf_op jit(solution)/shard_map/spread/pallas_call | solution.py:640
  511.0 4.6 copy-done
  515.5 65.2 %multiply_subtract_fusion = (f32[6297600]{0:T(1024)}, f32[6297600]{0:T(1024)}, f32[6297600]{0:T(1024)}, f32[6297600]{0:T(1024)}) fusion(f32[6297600]{0:T(1024)} %param.9, f32[6297600]{0:T(1024)} %param.10, f32[6297600]{0:T(1024)} %param.11, s32[]{:T(128)S(6)} %select_n.35, bf16[96,128]{1,0:T(8,128)(2,1)S(1)} %fusion.41, bf16[49152,128]{1,0:T(8,128)(2,1)} %bitcast.113), kind=kLoop, calls=%fused_computation.2 | loop fusion | flops 125952000 | bytes 188940288 | tf_op jit(solution)/shard_map/sub | solution.py:284
  (51 shorter events, 0.2 us)
Async XLA Ops:
  148.1 5.1 copy-start.6
  153.2 10.1 %copy-start.3 = (bf16[1024,1024]{1,0:T(8,128)(2,1)}, bf16[1024,1024]{1,0:T(8,128)(2,1)S(1)}, u32[]{:S(2)}) copy-start(bf16[1024,1024]{1,0:T(8,128)(2,1)S(1)} %reshape.267) | copy-start | bytes 6291460
  163.1 7.7 %copy-start.5 = (f32[16,128,128]{1,2,0:T(8,128)}, f32[16,128,128]{1,2,0:T(8,128)S(1)}, u32[]{:S(2)}) copy-start(f32[16,128,128]{1,2,0:T(8,128)S(1)} %get-tuple-element.46) | copy-start | bytes 3145732
  166.3 6.9 %copy-start.2 = (bf16[1024,1024]{1,0:T(8,128)(2,1)}, bf16[1024,1024]{1,0:T(8,128)(2,1)S(1)}, u32[]{:S(2)}) copy-start(bf16[1024,1024]{1,0:T(8,128)(2,1)S(1)} %reshape.263) | copy-start | bytes 6291460
  170.8 2.5 copy-start.14
  191.3 5.3 copy-start.12
  191.3 6.7 %copy-start.1 = (bf16[4096,1024]{1,0:T(8,128)(2,1)S(1)}, bf16[4096,1024]{1,0:T(8,128)(2,1)}, u32[]{:S(2)}) copy-start(bf16[4096,1024]{1,0:T(8,128)(2,1)} %reshape.271) | copy-start | bytes 25165828
  196.9 4.5 slice-start
  198.0 3.5 copy-start.7
  198.0 3.5 slice-start.1
  201.4 4.9 copy-start.9
  201.4 3.3 copy-start.4
  218.9 8.3 %copy-start.10 = (bf16[128,4096]{1,0:T(8,128)(2,1)S(1)}, bf16[128,4096]{1,0:T(8,128)(2,1)}, u32[]{:S(2)}) copy-start(bf16[128,4096]{1,0:T(8,128)(2,1)} %copy-done.9) | copy-start | bytes 3145732
  233.1 18.5 %copy-start.13 = (bf16[16,64,128]{2,1,0:T(8,128)(2,1)S(1)}, bf16[16,64,128]{2,1,0:T(8,128)(2,1)}, u32[]{:S(2)}) copy-start(bf16[16,64,128]{2,1,0:T(8,128)(2,1)} %convolution_convert_fusion.1) | copy-start | bytes 786436
  233.1 20.6 %copy-start.11 = (bf16[128,16,64]{0,2,1:T(8,128)(2,1)S(1)}, bf16[128,16,64]{0,2,1:T(8,128)(2,1)}, u32[]{:S(2)}) copy-start(bf16[128,16,64]{0,2,1:T(8,128)(2,1)} %get-tuple-element.42) | copy-start | bytes 786436
  258.7 7.8 %copy-start.8 = (f32[128,1024]{1,0:T(8,128)S(1)}, f32[128,1024]{1,0:T(8,128)}, u32[]{:S(2)}) copy-start(f32[128,1024]{1,0:T(8,128)} %copy-done.7) | copy-start | bytes 1572868
  511.0 4.6 copy-start
